TPU v7x, 32 devices: a whole 2x2x4 slice. The times are simulated.
32 devices in a mesh: seq: 4 (over z), wt: 8 (over y, x, core).
Axes of the slice: x: 2, y: 2, z: 4, core: 2. Of those that a mesh axis runs over, the one named last changes fastest.
Arguments:
- tokens_in: bfloat16 [896, 4608], P('seq', 'wt'), may hold values from -6 to 6
- norm_gain: float32 [4608], P('wt'), may hold values from 0.25 to 1.75
- positions: int32 [896], P('seq'), may hold values from 0 to 671, as said below
- blocks: bfloat16 [8, 16, 128, 128], P('wt'), may hold values from -0.125 to 0.125
- slot_code: int32 [8, 16], P('wt'), may hold values from -1 to 575, as said below
- out_grad: bfloat16 [896, 1024], P('seq', 'wt'), may hold values from -6 to 6
Outputs:
- attn_out: bfloat16 [896, 1024], P('seq', 'wt')
- tokens_grad: bfloat16 [896, 4608], P('seq', 'wt')
- gain_grad: float32 [4608], P('wt')
- block_grads: bfloat16 [8, 16, 128, 128], P('wt')
Inputs may be any that keep to these rules, and one draw needn't show every extreme that they name: Positions count the tokens of each document from 0: positions[0] = 0 and every later entry is either 0 (a new document starts) or the entry before plus one. The longest document has exactly 672 tokens. slot_code[o, s] is -1 for an empty slot, else u * 2 * 36 + p with head u and 0 <= p < 72; no value other than -1 appears twice. One owner holds at most 2 blocks for one head; in every draw some owner holds 2 blocks for every head and some head has 2 blocks at every owner.
All inputs are finite; a program needn't handle non-finite values.
Results may differ from a plain program's by a relative error of at most 0.023.
Values may be sent and summed in bfloat16 or wider, within the bound.
A program may use at most 64 MiB of HBM per device.

v0:
```python
import jax
import jax.numpy as jnp
from jax import lax
from jax.sharding import PartitionSpec as P

D = 4608
HD = 128
BLK = 128
CAP = 2


query_scale = 144.0 ** (-0.5)
soft_cap = 50.0
norm_eps = 1e-06


def from_partner(block, axis, stride):
    count = lax.axis_size(axis)
    route = []
    for low in range(count):
        high = low | 1 << stride
        if high != low and high < count:
            route += [(low, high), (high, low)]
    return lax.ppermute(block, axis, route)


def shifted(value, axis, steps):
    count = lax.axis_size(axis)
    initial, last = (max(0, -steps), min(count, count - steps))
    return lax.ppermute(value, axis, [(source, source + steps) for source in range(initial, last)])


def rope_tables(positions, head_width):
    half_width = head_width // 2
    frequency = 10000.0 ** (-2.0 * jnp.arange(half_width, dtype=jnp.float32) / head_width)
    angles = positions.astype(jnp.float32)[:, None] * frequency[None, :]
    return (jnp.cos(angles), jnp.sin(angles))


def rotate(vector, cos_table, sin_table):
    half_width = vector.shape[-1] // 2
    first_half = vector[..., :half_width]
    second_half = vector[..., half_width:]
    return jnp.concatenate(
        [
            first_half * cos_table - second_half * sin_table,
            first_half * sin_table + second_half * cos_table,
        ],
        axis=-1,
    )


def contract(left, right):
    return lax.dot_general(
        left, right, (((1,), (1,)), ((), ())), preferred_element_type=jnp.float32
    )


def contract_rows(left, right):
    return lax.dot_general(
        left, right, (((0,), (0,)), ((), ())), preferred_element_type=jnp.float32
    )


def body(tokens_in, norm_gain, positions, blocks, slot_code, out_grad):
    tok_rows = tokens_in.shape[0]
    groups = lax.axis_size("wt")
    slab_index = lax.axis_index("seq")
    is_even = lax.axis_index("wt") % 2 == 0
    tokens_f32 = tokens_in.astype(jnp.float32)
    squares = lax.psum(jnp.sum(tokens_f32 * tokens_f32, axis=1), "wt")
    inv_rms = lax.rsqrt(squares / D + norm_eps)
    scaled = tokens_f32 * inv_rms[:, None]
    normed_part = (scaled * norm_gain[None, :]).astype(jnp.bfloat16)
    normed = lax.all_gather(normed_part, "wt", axis=1, tiled=True)
    pos_count = 2 * (D // BLK)
    row_blocks = pos_count // 2
    slot_codes = slot_code[0]
    is_live = slot_codes >= 0
    target_user = jnp.where(is_live, slot_codes // pos_count, 0)
    user_match = (
        (target_user[:, None] == jnp.arange(groups, dtype=jnp.int32)[None, :]) & is_live[:, None]
    ).astype(jnp.int32)
    earlier = jnp.cumsum(user_match, axis=0) - user_match
    slot_rank = jnp.sum(earlier * user_match, axis=1)
    dump_slot = groups * CAP
    slot_dest = jnp.where(is_live, target_user * CAP + slot_rank, dump_slot)
    block_place = (slot_codes - target_user * pos_count).astype(jnp.float32)
    outgoing = jnp.zeros((dump_slot + 1, BLK, BLK), jnp.bfloat16).at[slot_dest].set(blocks[0])
    outgoing_pos = (
        jnp.full((dump_slot + 1,), -1.0, jnp.float32)
        .at[slot_dest]
        .set(block_place)
        .astype(jnp.bfloat16)
    )
    arrived, arrived_pos = (
        lax.all_to_all(
            outgoing[:dump_slot].reshape(groups, CAP, BLK, BLK),
            "wt",
            split_axis=0,
            concat_axis=0,
            tiled=True,
        ),
        lax.all_to_all(
            outgoing_pos[:dump_slot].reshape(groups, CAP),
            "wt",
            split_axis=0,
            concat_axis=0,
            tiled=True,
        ),
    )
    arrival = arrived_pos.reshape(-1).astype(jnp.int32)
    arrival = jnp.where(arrival < 0, pos_count, arrival)
    weight_table = (
        jnp.zeros((pos_count + 1, BLK, BLK), jnp.bfloat16)
        .at[arrival]
        .set(arrived.reshape(-1, BLK, BLK))
    )
    w_query = weight_table[:row_blocks].reshape(D, HD)
    w_pair = weight_table[row_blocks:pos_count].reshape(D, HD)
    query_proj = jnp.dot(normed, w_query, preferred_element_type=jnp.float32)
    pair_proj = jnp.dot(normed, w_pair, preferred_element_type=jnp.float32)
    cos_table, sin_table = rope_tables(positions, HD)
    query_rot = (rotate(query_proj, cos_table, sin_table) * query_scale).astype(jnp.bfloat16)
    own_pair = jnp.where(is_even, rotate(pair_proj, cos_table, sin_table), pair_proj).astype(
        jnp.bfloat16
    )
    partner = from_partner(own_pair, "wt", 0)
    key_rows = jnp.where(is_even, own_pair, partner)
    value_rows = jnp.where(is_even, partner, own_pair)
    reach_slabs = lax.axis_size("seq") // 2
    window = reach_slabs * tok_rows
    key_list = [key_rows]
    value_list = [value_rows]
    for offset in range(1, reach_slabs + 1):
        prev_key, prev_value = shifted((key_rows, value_rows), "seq", offset)
        key_list.append(prev_key)
        value_list.append(prev_value)
    key_all = jnp.concatenate(key_list, axis=0)
    value_all = jnp.concatenate(value_list, axis=0)
    local_index = jnp.arange(tok_rows, dtype=jnp.int32)
    query_index = slab_index * tok_rows + local_index
    key_index = jnp.concatenate(
        [(slab_index - offset) * tok_rows + local_index for offset in range(reach_slabs + 1)]
    )
    doc_begin = query_index - positions
    distance = query_index[:, None] - key_index[None, :]
    visible = (distance >= 0) & (distance < window) & (key_index[None, :] >= doc_begin[:, None])
    scores = contract(query_rot, key_all)
    capped = soft_cap * jnp.tanh(scores / soft_cap)
    exp_scores = jnp.where(visible, jnp.exp(capped), 0.0)
    row_total = jnp.sum(exp_scores, axis=1)
    attn_rows = (
        jnp.dot(exp_scores.astype(jnp.bfloat16), value_all, preferred_element_type=jnp.float32)
        / row_total[:, None]
    ).astype(jnp.bfloat16)
    row_delta = jnp.sum(out_grad.astype(jnp.float32) * attn_rows.astype(jnp.float32), axis=1)
    soft_probs = exp_scores / row_total[:, None]
    prob_grad = contract(out_grad, value_all)
    score_grad = soft_probs * (prob_grad - row_delta[:, None]) * (1.0 - (capped / soft_cap) ** 2)
    score_low = score_grad.astype(jnp.bfloat16)
    probs_low = soft_probs.astype(jnp.bfloat16)
    rot_grad = jnp.dot(score_low, key_all, preferred_element_type=jnp.float32)
    query_grad = (rotate(rot_grad, cos_table, -sin_table) * query_scale).astype(jnp.bfloat16)
    key_grads = contract_rows(score_low, query_rot)
    value_grads = contract_rows(probs_low, out_grad)
    key_total = key_grads[:tok_rows]
    value_total = value_grads[:tok_rows]
    for offset in range(1, reach_slabs + 1):
        recv_key, recv_value = (
            shifted(
                key_grads[offset * tok_rows : (offset + 1) * tok_rows].astype(jnp.bfloat16),
                "seq",
                -offset,
            ).astype(jnp.float32),
            shifted(
                value_grads[offset * tok_rows : (offset + 1) * tok_rows].astype(jnp.bfloat16),
                "seq",
                -offset,
            ).astype(jnp.float32),
        )
        key_total = key_total + recv_key
        value_total = value_total + recv_value
    outbound = jnp.where(is_even, value_total, key_total)
    partner_grad = from_partner(outbound.astype(jnp.bfloat16), "wt", 0).astype(outbound.dtype)
    pair_total = jnp.where(is_even, key_total, value_total) + partner_grad
    pair_grad = jnp.where(is_even, rotate(pair_total, cos_table, -sin_table), pair_total).astype(
        jnp.bfloat16
    )
    normed_grad = (
        lax.psum_scatter(
            (contract(w_query, query_grad) + contract(w_pair, pair_grad)).astype(jnp.bfloat16),
            "wt",
            scatter_dimension=0,
            tiled=True,
        )
        .astype(jnp.float32)
        .T
    )
    scaled_grad = normed_grad * norm_gain[None, :]
    row_dots = lax.psum(jnp.sum(scaled_grad * scaled, axis=1), "wt")
    tokens_grad = (inv_rms[:, None] * (scaled_grad - scaled * (row_dots / D)[:, None])).astype(
        jnp.bfloat16
    )
    gain_part = jnp.sum(normed_grad * scaled, axis=0)
    grad_query = contract_rows(normed, query_grad)
    grad_pair = contract_rows(normed, pair_grad)
    grad_table = jnp.concatenate(
        [
            grad_query.reshape(row_blocks, BLK, BLK),
            grad_pair.reshape(row_blocks, BLK, BLK),
            jnp.zeros((1, BLK, BLK), jnp.float32),
        ],
        axis=0,
    )
    slot_grads = grad_table[arrival].reshape(groups, CAP, BLK, BLK)
    empty_block = jnp.zeros((1, BLK, BLK), jnp.bfloat16)
    returned = lax.all_to_all(
        slot_grads.astype(jnp.bfloat16), "wt", split_axis=0, concat_axis=0, tiled=True
    )
    owned_grads = jnp.concatenate([returned.reshape(-1, BLK, BLK), empty_block], axis=0)[slot_dest]
    summed = (
        lax.psum(owned_grads.astype(jnp.float32).astype(jnp.bfloat16), "seq").astype(jnp.float32),
        lax.psum(gain_part.astype(jnp.bfloat16), "seq").astype(jnp.float32),
    )
    block_grads = summed[0].astype(jnp.bfloat16)
    gain_total = summed[1]
    return (attn_rows, tokens_grad, gain_total, block_grads[None])


def solution(mesh):
    placed = (
        P("seq", "wt"),
        P("wt"),
        P("seq"),
        P("wt", None, None, None),
        P("wt", None),
        P("seq", "wt"),
    )
    return jax.shard_map(
        body,
        mesh=mesh,
        in_specs=placed,
        out_specs=(P("seq", "wt"), P("seq", "wt"), P("wt"), P("wt", None, None, None)),
        check_vma=False,
    )
```

profile of v0, /device:TPU:0, one launch (start us, length us, event | category | flops | bytes accessed | tf_op | source)
XLA Modules:
  0.0 198.3 jit_solution(12539337857385299882)
XLA Ops:
  7.2 1.1 fusion.19
  8.4 15.1 %psum.28 = f32[224]{0:T(256)S(1)} all-reduce(f32[224]{0:T(256)S(1)} %fusion.19), channel_id=1, replica_groups=mesh['seq'=4,'wt'=8] {'wt'}, use_global_device_ids=true, to_apply=%region_1.2 | all-reduce | flops 224 | bytes 1792 | tf_op jit(solution)/shard_map/psum | solution.py:71
  23.5 1.8 fusion.23
  25.3 0.7 bitcast_compare_fusion
  26.0 0.7 fusion.63
  26.8 0.2 select_reduce_fusion
  27.0 0.7 fusion.60
  27.7 0.6 scatter_custom_fusion
  28.3 0.7 all_to_all.16
  29.0 3.3 %all-to-all-start = ((bf16[8,1,2]{2,1,0:T(2,128)(2,1)}), bf16[8,1,2]{2,1,0:T(2,128)(2,1)S(1)}, u32[]{:S(2)}, u32[]{:S(2)}) async-start(bf16[8,1,2]{2,1,0:T(2,128)(2,1)} %all_to_all.16), calls=%async_computation | async-start | bytes 8192 | tf_op jit(solution)/shard_map/all_to_all | solution.py:104
  32.4 1.1 scatter_fusion
  33.6 0.8 slice.80
  34.4 2.4 %all-to-all-done = bf16[8,1,2]{2,1,0:T(2,128)(2,1)S(1)} async-done(((bf16[8,1,2]{2,1,0:T(2,128)(2,1)}), bf16[8,1,2]{2,1,0:T(2,128)(2,1)S(1)}, u32[]{:S(2)}, u32[]{:S(2)}) %all-to-all-start) | async-done | bytes 64 | tf_op jit(solution)/shard_map/all_to_all | solution.py:104
  36.8 3.5 %all-to-all-start.1 = ((bf16[8,2,128,128]{3,2,1,0:T(8,128)(2,1)}), bf16[8,2,128,128]{3,2,1,0:T(8,128)(2,1)S(1)}, u32[]{:S(2)}, u32[]{:S(2)}) async-start(bf16[8,2,128,128]{3,2,1,0:T(8,128)(2,1)} %bitcast.10), calls=%async_computation.1 | async-start | bytes 1048576 | tf_op jit(solution)/shard_map/all_to_all | solution.py:97
  40.6 12.9 %all-to-all-done.1 = bf16[8,2,128,128]{3,2,1,0:T(8,128)(2,1)S(1)} async-done(((bf16[8,2,128,128]{3,2,1,0:T(8,128)(2,1)}), bf16[8,2,128,128]{3,2,1,0:T(8,128)(2,1)S(1)}, u32[]{:S(2)}, u32[]{:S(2)}) %all-to-all-start.1) | async-done | bytes 524320 | tf_op jit(solution)/shard_map/all_to_all | solution.py:97
  53.5 2.0 %broadcast_in_dim.18 = bf16[73,128,128]{2,1,0:T(8,128)(2,1)} broadcast(bf16[]{:T(256)} %constant.70.clone.1), dimensions={} | broadcast | bytes 2392066 | tf_op jit(solution)/shard_map/broadcast_in_dim | solution.py:115
  55.5 2.7 %scatter_fusion.1 = bf16[73,128,128]{2,1,0:T(8,128)(2,1)} fusion(bf16[73,128,128]{2,1,0:T(8,128)(2,1)} %broadcast_in_dim.18, s32[16]{0:T(128)S(1)} %fusion.61, bf16[16,128,128]{2,1,0:T(8,128)(2,1)S(1)} %bitcast.109), kind=kCustom, calls=%fused_computation.4 | custom fusion | bytes 1572928 | tf_op jit(solution)/shard_map/scatter | solution.py:117
  58.2 2.9 %fusion.73 = (bf16[36,128,128]{2,1,0:T(8,128)(2,1)S(1)}, bf16[36,128,128]{2,1,0:T(8,128)(2,1)}) fusion(bf16[73,128,128]{2,1,0:T(8,128)(2,1)} %scatter_fusion.1), kind=kLoop, calls=%fused_computation.127 | loop fusion | bytes 4718592 | tf_op jit(solution)/shard_map/slice | solution.py:119
  61.1 3.8 %copy.13 = bf16[8,576,224]{1,0,2:T(8,128)(2,1)} copy(bf16[8,576,224]{1,2,0:T(8,128)(2,1)} %all-gather.3.cloned.1.call-done) | data formatting | bytes 4128768 | tf_op jit(solution)/shard_map/all_gather | solution.py:75
  64.9 3.4 %reshape.231 = bf16[4608,224]{0,1:T(8,128)(2,1)S(1)} reshape(bf16[8,576,224]{1,0,2:T(8,128)(2,1)} %copy.13) | data formatting | bytes 4128768
  68.4 2.0 fusion.79
  70.3 0.7 fusion.78
  71.0 0.5 fusion.47
  71.7 0.5 fusion.45
  72.2 0.7 collective-permute-done
  73.0 4.7 %collective-permute-start.2 = (bf16[224,128]{1,0:T(8,128)(2,1)S(1)}, bf16[224,128]{1,0:T(8,128)(2,1)S(1)}, u32[]{:S(2)}, u32[]{:S(2)}) collective-permute-start(bf16[224,128]{1,0:T(8,128)(2,1)S(1)} %get-tuple-element.22), channel_id=1, source_target_pairs={{0,16},{8,24},{1,17},{9,25},{2,18},{10,26},{3,19},{11,27},{4,20},{... | collective-permute-start | bytes 172040 | tf_op jit(solution)/shard_map/ppermute | solution.py:30
  77.7 3.6 %collective-permute-start.1 = (bf16[224,128]{1,0:T(8,128)(2,1)S(1)}, bf16[224,128]{1,0:T(8,128)(2,1)S(1)}, u32[]{:S(2)}, u32[]{:S(2)}) collective-permute-start(bf16[224,128]{1,0:T(8,128)(2,1)S(1)} %get-tuple-element.22), channel_id=1, source_target_pairs={{0,8},{8,16},{16,24},{1,9},{9,17},{17,25},{2,10},{10,18},{18,26},{... | collective-permute-start | bytes 172040 | tf_op jit(solution)/shard_map/ppermute | solution.py:30
  81.3 1.3 collective-permute-start.4
  82.6 1.9 collective-permute-start.3
  84.6 0.6 fusion.71
  85.2 0.5 fusion.77
  85.7 1.3 collective-permute-start.7
  87.0 1.3 collective-permute-start.8
  88.3 1.0 multiply_reduce_fusion
  89.3 0.5 fusion.5
  89.8 0.3 fusion.76
  90.1 1.3 collective-permute-start.5
  91.4 1.5 collective-permute-start.6
  92.9 0.2 fusion.55
  93.2 0.5 fusion.41
  93.8 0.8 collective-permute-done.8
  94.6 2.3 %collective-permute-done.5 = bf16[224,128]{1,0:T(8,128)(2,1)S(1)} collective-permute-done((bf16[224,128]{1,0:T(8,128)(2,1)S(1)}, bf16[224,128]{1,0:T(8,128)(2,1)S(1)}, u32[]{:S(2)}, u32[]{:S(2)}) %collective-permute-start.5) | collective-permute-done | bytes 57376 | tf_op jit(solution)/shard_map/ppermute | solution.py:30
  96.8 3.3 %collective-permute-done.6 = bf16[224,128]{1,0:T(8,128)(2,1)S(1)} collective-permute-done((bf16[224,128]{1,0:T(8,128)(2,1)S(1)}, bf16[224,128]{1,0:T(8,128)(2,1)S(1)}, u32[]{:S(2)}, u32[]{:S(2)}) %collective-permute-start.6) | collective-permute-done | bytes 57376 | tf_op jit(solution)/shard_map/ppermute | solution.py:30
  100.3 0.7 fusion.80
  101.0 0.5 collective-permute-done.9
  101.6 0.5 fusion.43
  102.3 2.0 %fusion = bf16[4608,224]{0,1:T(8,128)(2,1)} fusion(f32[4608,224]{0,1:T(8,128)S(1)} %fusion.80, bf16[4608,128]{1,0:T(8,128)(2,1)S(1)} %bitcast.106, bf16[224,128]{1,0:T(8,128)(2,1)S(1)} %fusion.54), kind=kOutput, calls=%fused_computation.6 | convolution fusion | flops 266305536 | bytes 7430144 | tf_op jit(solution)/shard_map/dot_general | solution.py:54
  104.3 4.1 %copy.17 = bf16[4608,224]{1,0:T(8,128)(2,1)} copy(bf16[4608,224]{0,1:T(8,128)(2,1)} %fusion) | data formatting | bytes 4128768
  108.5 0.8 fusion.81
  109.4 0.8 fusion.82
  110.2 0.3 maximum_maximum_fusion
  110.5 1.4 gather_fusion
  111.9 3.6 %all-to-all-start.2 = ((bf16[8,2,128,128]{3,2,1,0:T(8,128)(2,1)}), bf16[8,2,128,128]{3,2,1,0:T(8,128)(2,1)S(1)}, u32[]{:S(2)}, u32[]{:S(2)}) async-start(bf16[8,2,128,128]{3,2,1,0:T(8,128)(2,1)} %bitcast.18), calls=%async_computation.2 | async-start | bytes 1048576 | tf_op jit(solution)/shard_map/all_to_all | solution.py:218
  115.6 9.6 %all-to-all-done.2 = bf16[8,2,128,128]{3,2,1,0:T(8,128)(2,1)S(1)} async-done(((bf16[8,2,128,128]{3,2,1,0:T(8,128)(2,1)}), bf16[8,2,128,128]{3,2,1,0:T(8,128)(2,1)S(1)}, u32[]{:S(2)}, u32[]{:S(2)}) %all-to-all-start.2) | async-done | bytes 524320 | tf_op jit(solution)/shard_map/all_to_all | solution.py:218
  125.3 1.4 gather_fusion.1
  126.7 21.8 %reduce-scatter.4.cloned.1.call-done = bf16[576,224]{1,0:T(8,128)(2,1)} async-done(((bf16[4608,224]{1,0:T(8,128)(2,1)}), bf16[576,224]{1,0:T(8,128)(2,1)}) %reduce-scatter.4.cloned.1.call-update) | async-done | bytes 258064
  148.5 1.1 copy.18
  149.7 0.4 fusion.18
  150.1 11.7 %psum.30 = bf16[576]{0:T(1024)(128)(2,1)S(1)} all-reduce(bf16[576]{0:T(1024)(128)(2,1)S(1)} %get-tuple-element.4), channel_id=1, replica_groups=mesh['seq'=4,'wt'=8] {'seq'}, use_global_device_ids=true, to_apply=%region_13.14 | all-reduce | flops 576 | bytes 2304 | tf_op jit(solution)/shard_map/psum | solution.py:224
  161.8 0.6 convert_element_type.133
  162.4 12.2 %psum.29 = f32[224]{0:T(256)S(1)} all-reduce(f32[224]{0:T(256)S(1)} %get-tuple-element.5), channel_id=1, replica_groups=mesh['seq'=4,'wt'=8] {'wt'}, use_global_device_ids=true, to_apply=%region_11.12 | all-reduce | flops 224 | bytes 1792 | tf_op jit(solution)/shard_map/psum | solution.py:201
  174.6 0.9 fusion.17
  175.5 14.4 %all-reduce.3.cloned.1.call-done = bf16[1,16,128,128]{3,2,1,0:T(8,128)(2,1)} async-done(((bf16[1,16,128,128]{3,2,1,0:T(8,128)(2,1)}), bf16[1,16,128,128]{3,2,1,0:T(8,128)(2,1)}) %all-reduce.3.cloned.1.call-update) | async-done | bytes 524304 | tf_op jit(solution)/shard_map/psum | solution.py:223
  189.9 1.9 copy.22
  (53 shorter events, 1.5 us)
Async XLA Ops:
  7.2 25.3 %copy-start.2 = (bf16[1,16,128,128]{3,2,1,0:T(8,128)(2,1)S(1)}, bf16[1,16,128,128]{3,2,1,0:T(8,128)(2,1)}, u32[]{:S(2)}) copy-start(bf16[1,16,128,128]{3,2,1,0:T(8,128)(2,1)} %param.9) | copy-start | bytes 1572868
  7.2 53.9 %all-gather.3.cloned.1.call-start = ((), (), s32[]{:S(2)}) async-start(), calls=%async_computation.5 | async-start | bytes 2580480 | tf_op jit(solution)/shard_map/all_gather | solution.py:75
  23.5 10.9 %copy-start.4 = (s32[224]{0:T(256)S(1)}, s32[224]{0:T(256)}, u32[]{:S(2)}) copy-start(s32[224]{0:T(256)} %param.8) | copy-start | bytes 2692
  29.0 7.8 %all-to-all-start = ((bf16[8,1,2]{2,1,0:T(2,128)(2,1)}), bf16[8,1,2]{2,1,0:T(2,128)(2,1)S(1)}, u32[]{:S(2)}, u32[]{:S(2)}) async-start(bf16[8,1,2]{2,1,0:T(2,128)(2,1)} %all_to_all.16), calls=%async_computation | async-start | bytes 8192 | tf_op jit(solution)/shard_map/all_to_all | solution.py:104
  36.8 16.7 %all-to-all-start.1 = ((bf16[8,2,128,128]{3,2,1,0:T(8,128)(2,1)}), bf16[8,2,128,128]{3,2,1,0:T(8,128)(2,1)S(1)}, u32[]{:S(2)}, u32[]{:S(2)}) async-start(bf16[8,2,128,128]{3,2,1,0:T(8,128)(2,1)} %bitcast.10), calls=%async_computation.1 | async-start | bytes 1048576 | tf_op jit(solution)/shard_map/all_to_all | solution.py:97
  40.3 108.2 %reduce-scatter.4.cloned.1.call-start = ((), (), s32[]{:S(2)}) async-start(), calls=%async_computation.6 | async-start | bytes 2654208
  71.0 14.1 %copy-start.5 = (bf16[224,128]{1,0:T(8,128)(2,1)S(1)}, bf16[224,128]{1,0:T(8,128)(2,1)}, u32[]{:S(2)}) copy-start(bf16[224,128]{1,0:T(8,128)(2,1)} %param.11) | copy-start | bytes 172036
  71.6 1.3 collective-permute-start
  73.0 11.6 %collective-permute-start.2 = (bf16[224,128]{1,0:T(8,128)(2,1)S(1)}, bf16[224,128]{1,0:T(8,128)(2,1)S(1)}, u32[]{:S(2)}, u32[]{:S(2)}) collective-permute-start(bf16[224,128]{1,0:T(8,128)(2,1)S(1)} %get-tuple-element.22), channel_id=1, source_target_pairs={{0,16},{8,24},{1,17},{9,25},{2,18},{10,26},{3,19},{11,27},{4,20},{... | collective-permute-start | bytes 172040 | tf_op jit(solution)/shard_map/ppermute | solution.py:30
  77.7 6.9 %collective-permute-start.1 = (bf16[224,128]{1,0:T(8,128)(2,1)S(1)}, bf16[224,128]{1,0:T(8,128)(2,1)S(1)}, u32[]{:S(2)}, u32[]{:S(2)}) collective-permute-start(bf16[224,128]{1,0:T(8,128)(2,1)S(1)} %get-tuple-element.22), channel_id=1, source_target_pairs={{0,8},{8,16},{16,24},{1,9},{9,17},{17,25},{2,10},{10,18},{18,26},{... | collective-permute-start | bytes 172040 | tf_op jit(solution)/shard_map/ppermute | solution.py:30
  81.3 7.0 %collective-permute-start.4 = (bf16[224,128]{1,0:T(8,128)(2,1)S(1)}, bf16[224,128]{1,0:T(8,128)(2,1)S(1)}, u32[]{:S(2)}, u32[]{:S(2)}) collective-permute-start(bf16[224,128]{1,0:T(8,128)(2,1)S(1)} %get-tuple-element.23), channel_id=1, source_target_pairs={{0,16},{8,24},{1,17},{9,25},{2,18},{10,26},{3,19},{11,27},{4,20},{... | collective-permute-start | bytes 172040 | tf_op jit(solution)/shard_map/ppermute | solution.py:30
  82.6 5.7 %collective-permute-start.3 = (bf16[224,128]{1,0:T(8,128)(2,1)S(1)}, bf16[224,128]{1,0:T(8,128)(2,1)S(1)}, u32[]{:S(2)}, u32[]{:S(2)}) collective-permute-start(bf16[224,128]{1,0:T(8,128)(2,1)S(1)} %get-tuple-element.23), channel_id=1, source_target_pairs={{0,8},{8,16},{16,24},{1,9},{9,17},{17,25},{2,10},{10,18},{18,26},{... | collective-permute-start | bytes 172040 | tf_op jit(solution)/shard_map/ppermute | solution.py:30
  85.7 8.1 %collective-permute-start.7 = (bf16[224,128]{1,0:T(8,128)(2,1)S(1)}, bf16[224,128]{1,0:T(8,128)(2,1)S(1)}, u32[]{:S(2)}, u32[]{:S(2)}) collective-permute-start(bf16[224,128]{1,0:T(8,128)(2,1)S(1)} %get-tuple-element.10), channel_id=1, source_target_pairs={{8,0},{16,8},{24,16},{9,1},{17,9},{25,17},{10,2},{18,10},{26,18},{... | collective-permute-start | bytes 172040 | tf_op jit(solution)/shard_map/ppermute | solution.py:30
  87.0 7.6 %collective-permute-start.8 = (bf16[224,128]{1,0:T(8,128)(2,1)S(1)}, bf16[224,128]{1,0:T(8,128)(2,1)S(1)}, u32[]{:S(2)}, u32[]{:S(2)}) collective-permute-start(bf16[224,128]{1,0:T(8,128)(2,1)S(1)} %get-tuple-element.11), channel_id=1, source_target_pairs={{16,0},{24,8},{17,1},{25,9},{18,2},{26,10},{19,3},{27,11},{20,4},{... | collective-permute-start | bytes 172040 | tf_op jit(solution)/shard_map/ppermute | solution.py:30
  90.1 6.7 %collective-permute-start.5 = (bf16[224,128]{1,0:T(8,128)(2,1)S(1)}, bf16[224,128]{1,0:T(8,128)(2,1)S(1)}, u32[]{:S(2)}, u32[]{:S(2)}) collective-permute-start(bf16[224,128]{1,0:T(8,128)(2,1)S(1)} %get-tuple-element.12), channel_id=1, source_target_pairs={{8,0},{16,8},{24,16},{9,1},{17,9},{25,17},{10,2},{18,10},{26,18},{... | collective-permute-start | bytes 172040 | tf_op jit(solution)/shard_map/ppermute | solution.py:30
  91.4 8.7 %collective-permute-start.6 = (bf16[224,128]{1,0:T(8,128)(2,1)S(1)}, bf16[224,128]{1,0:T(8,128)(2,1)S(1)}, u32[]{:S(2)}, u32[]{:S(2)}) collective-permute-start(bf16[224,128]{1,0:T(8,128)(2,1)S(1)} %get-tuple-element.13), channel_id=1, source_target_pairs={{16,0},{24,8},{17,1},{25,9},{18,2},{26,10},{19,3},{27,11},{20,4},{... | collective-permute-start | bytes 172040 | tf_op jit(solution)/shard_map/ppermute | solution.py:30
  100.2 1.3 collective-permute-start.9
  101.0 1.3 copy-start
  111.9 37.8 %copy-start.1 = (bf16[224,576]{1,0:T(8,128)(2,1)S(1)}, bf16[224,576]{1,0:T(8,128)(2,1)}, u32[]{:S(2)}) copy-start(bf16[224,576]{1,0:T(8,128)(2,1)} %param.6) | copy-start | bytes 774148
  111.9 37.8 %copy-start.3 = (f32[576]{0:T(1024)S(1)}, f32[576]{0:T(1024)}, u32[]{:S(2)}) copy-start(f32[576]{0:T(1024)} %param.7) | copy-start | bytes 6916
  111.9 13.3 %all-to-all-start.2 = ((bf16[8,2,128,128]{3,2,1,0:T(8,128)(2,1)}), bf16[8,2,128,128]{3,2,1,0:T(8,128)(2,1)S(1)}, u32[]{:S(2)}, u32[]{:S(2)}) async-start(bf16[8,2,128,128]{3,2,1,0:T(8,128)(2,1)} %bitcast.18), calls=%async_computation.2 | async-start | bytes 1048576 | tf_op jit(solution)/shard_map/all_to_all | solution.py:218
  115.6 74.3 %all-reduce.3.cloned.1.call-start = ((), (), s32[]{:S(2)}) async-start(), calls=%async_computation.4 | async-start | bytes 1048576 | tf_op jit(solution)/shard_map/psum | solution.py:223
Sparse Core Ops, SparseCore 0:
  25.5 31.3 all-gather.2
  108.6 39.9 reduce-scatter.3
  151.6 38.2 all-reduce.2
where the time goes:
time: 199 us; the launch traced here: 198 us
  waiting for transfers between devices  68.7 us (35%)
  blocking collectives  39 us (20%)
  local copies, waits for them, and re-layouts  28.5 us (14%)
  starting transfers between devices  27.5 us (14%)
  between operations  14.2 us (7%)
  matrix products  10.2 us (5%)
  other arithmetic  10.1 us (5%)
    unnamed x4, waiting for transfers between devices  21.9 us
    ppermute x8, starting transfers between devices, shifted(): lax.ppermute(value, axis, [(source, source + steps) for source in range(i...  16.8 us
    psum x1, blocking collectives, body(): squares = lax.psum(jnp.sum(tokens_f32 * tokens_f32, axis=1), 'wt')  15.1 us
    psum x1, waiting for transfers between devices, body(): lax.psum(owned_grads.astype(jnp.float32).astype(jnp.bfloat16), 'seq')  14.4 us
    all_to_all x1, waiting for transfers between devices, body(): lax.all_to_all(outgoing[:dump_slot].reshape(groups, CAP, BLK, BLK), 'wt',...  12.9 us
    psum x1, blocking collectives, body(): row_dots = lax.psum(jnp.sum(scaled_grad * scaled, axis=1), 'wt')  12.2 us
    psum x1, blocking collectives, body(): lax.psum(gain_part.astype(jnp.bfloat16), 'seq').astype(jnp.float32)  11.7 us
    unnamed x16, local copies, waits for them, and re-layouts  10.7 us
  transfers between devices with their start and end apart: 16, of which 10 were waited for; matrix products, arithmetic and copies ran while one was open for 13% of the time, Pallas kernels for 0%

commit v1 on v0

v1 whole, which is shorter than its diff:
```python
import functools
import jax
import jax.numpy as jnp
from jax import lax
from jax.experimental import pallas as pl
from jax.experimental.pallas import tpu as pltpu
from jax.sharding import PartitionSpec as P

D = 4608
HD = 128
BLK = 128
CAP = 2
RB = D // BLK
POS = 2 * RB
TP = 256

query_scale = 144.0 ** (-0.5)
soft_cap = 50.0
norm_eps = 1e-06

MESH = pl.DeviceIdType.MESH
F32 = jnp.float32
BF16 = jnp.bfloat16


def dot(left, right, ldim, rdim):
    return lax.dot_general(
        left, right, (((ldim,), (rdim,)), ((), ())), preferred_element_type=F32
    )


def rot(v, c, s):
    return v * c + jnp.concatenate([v[:, HD // 2 :], v[:, : HD // 2]], axis=1) * s


def kernel(
    n_seq, n_wt,
    tok, gain, pos, cos, sin, blocks, slot_of, dest, place, og,
    attn, tg, gg, bg,
    tf, tokT, scT, ngT, sq, rd, nT, stage, arrived, arrp, invv, inv_sm, arrp_sm, wd, proj,
    kv, kvs, kvr, cot, wz, wzr, ws, fin, gs, gr, gb, nblk,
    sq_s, sq_r, pc_s, pc_r, bl_s, bl_r, nt_s, nt_r, kv_s, kv_r, kg_s, kg_r,
    wz_s, wz_r, ow_s, ow_r, fi_s, fi_r, g_s, g_r, rd_s, rd_r, gb_s, gb_r, loc,
):
    t_rows, feats = tok.shape
    slots = blocks.shape[0]
    fp = tf.shape[1]
    count = n_wt * CAP
    reach = n_seq // 2
    window = reach * t_rows
    chunk = CAP * BLK // n_seq
    z = lax.axis_index("seq")
    w = lax.axis_index("wt")
    par = lax.rem(w, 2)
    even = par == 0
    partner = w + 1 - 2 * par
    c_tab = cos[...]
    s_tab = sin[...]
    pending = []

    def send(src, dst, ss, rs, device):
        copy = pltpu.make_async_remote_copy(
            src_ref=src, dst_ref=dst, send_sem=ss, recv_sem=rs, device_id=device, device_id_type=MESH
        )
        copy.start()
        return copy

    def recv(dst, ss, rs):
        pltpu.make_async_remote_copy(
            src_ref=dst, dst_ref=dst, send_sem=ss, recv_sem=rs, device_id=(z, partner), device_id_type=MESH
        ).wait_recv()

    def to_wt(d):
        return lax.rem(w + d, n_wt)

    def from_wt(d):
        return lax.rem(w + n_wt - d, n_wt)

    def to_seq(d):
        return lax.rem(z + d, n_seq)

    def from_seq(d):
        return lax.rem(z + n_seq - d, n_seq)

    def frows(index):
        return pl.ds(pl.multiple_of(index * feats, 16), feats)

    barrier = pltpu.get_barrier_semaphore()
    for d in range(1, n_wt):
        pl.semaphore_signal(barrier, inc=1, device_id=(z, to_wt(d)), device_id_type=MESH)
    for d in range(1, n_seq):
        for other in (w, partner):
            pl.semaphore_signal(barrier, inc=1, device_id=(to_seq(d), other), device_id_type=MESH)

    tf[...] = jnp.zeros_like(tf)
    tf[:t_rows, :feats] = tok[...].astype(F32)
    turned = tf[...].T
    tokT[...] = turned
    sq[0] = jnp.broadcast_to(jnp.sum(turned * turned, axis=0, keepdims=True), (8, TP))
    for k in range(count):
        stage[k] = blocks[slot_of[k]]
    pl.semaphore_wait(barrier, n_wt - 1 + 2 * (n_seq - 1))

    for d in range(1, n_wt):
        pending.append(send(sq.at[0], sq.at[d], sq_s.at[d], sq_r.at[d], (z, to_wt(d))))
    for d in range(1, n_wt):
        u = to_wt(d)
        pending.append(send(place.at[u], arrp.at[w], pc_s.at[d], pc_r.at[d], (z, u)))
    for d in range(1, n_wt):
        u = to_wt(d)
        pending.append(
            send(stage.at[pl.ds(u * CAP, CAP)], arrived.at[pl.ds(w * CAP + 1, CAP)], bl_s.at[d], bl_r.at[d], (z, u))
        )
    arrp[w] = place[w]
    arrived[0] = jnp.zeros((BLK, BLK), BF16)
    for r in range(CAP):
        arrived[w * CAP + 1 + r] = stage[w * CAP + r]

    for d in range(1, n_wt):
        recv(sq.at[d], sq_s.at[d], sq_r.at[d])
    total = sq[0]
    for d in range(1, n_wt):
        total = total + sq[d]
    inv_row = lax.rsqrt(total / D + norm_eps)[0:1, :]
    scaled = tokT[:feats, :] * inv_row
    scT[...] = scaled
    nT[frows(w), :] = (scaled * gain[...]).astype(BF16)
    for d in range(1, n_wt):
        pending.append(send(nT.at[frows(w)], nT.at[frows(w)], nt_s.at[d], nt_r.at[d], (z, to_wt(d))))

    for d in range(1, n_wt):
        recv(arrp.at[from_wt(d)], pc_s.at[d], pc_r.at[d])
    lane = lax.broadcasted_iota(jnp.int32, (8, 128), 1)
    index = jnp.zeros((8, 128), jnp.int32)
    for o in range(n_wt):
        for r in range(CAP):
            index = jnp.where(arrp[o, r : r + 1, :] == lane, o * CAP + r + 1, index)
    invv[...] = index
    one = pltpu.make_async_copy(invv, inv_sm, loc.at[0])
    two = pltpu.make_async_copy(arrp, arrp_sm, loc.at[1])
    one.start()
    two.start()
    one.wait()
    two.wait()
    for d in range(1, n_wt):
        recv(arrived.at[pl.ds(from_wt(d) * CAP + 1, CAP)], bl_s.at[d], bl_r.at[d])
    for p in range(RB):
        wd[p * BLK : (p + 1) * BLK, :BLK] = arrived[inv_sm[0, p]]
        wd[p * BLK : (p + 1) * BLK, BLK:] = arrived[inv_sm[0, RB + p]]

    proj[...] = dot(nT[frows(w), :], wd[frows(w), :], 0, 0)
    for d in range(1, n_wt):
        src = from_wt(d)
        recv(nT.at[frows(src)], nt_s.at[d], nt_r.at[d])
        proj[...] += dot(nT[frows(src), :], wd[frows(src), :], 0, 0)

    query = (rot(proj[:t_rows, :HD], c_tab, s_tab) * query_scale).astype(BF16)
    pair = proj[:t_rows, HD:]
    kv[0, par] = jnp.where(even, rot(pair, c_tab, s_tab), pair).astype(BF16)

    kv_out = []

    def kv_send(off, which):
        device = (z + off, w if which == 0 else partner)
        return pltpu.make_async_remote_copy(
            src_ref=kv.at[0, par], dst_ref=kv.at[off, par], send_sem=kv_s.at[off * 2 + which],
            recv_sem=kv_r.at[off * 2 + which], device_id=device, device_id_type=MESH,
        )

    pending.append(kv_send(0, 1))
    pending[-1].start()
    for off in range(1, reach + 1):

        @pl.when(z + off < n_seq)
        def _():
            kv_send(off, 0).start()
            kv_send(off, 1).start()

        @pl.when(z < off)
        def _():
            kv[off] = jnp.zeros((2, t_rows, HD), BF16)

    for p in range(RB):
        nblk[p] = nT[p * BLK : (p + 1) * BLK, :]
    fin[n_seq * n_wt] = jnp.zeros((chunk, BLK), BF16)
    out_grad = og[...]
    recv(kv.at[0, 1 - par], kv_s.at[1], kv_r.at[1])
    for off in range(1, reach + 1):

        @pl.when(z >= off)
        def _():
            recv(kv.at[off, par], kv_s.at[off * 2], kv_r.at[off * 2])
            recv(kv.at[off, 1 - par], kv_s.at[off * 2 + 1], kv_r.at[off * 2 + 1])

    gap = lax.broadcasted_iota(jnp.int32, (t_rows, t_rows), 0) - lax.broadcasted_iota(
        jnp.int32, (t_rows, t_rows), 1
    )
    limit = jnp.minimum(pos[...], window - 1)
    exps, tanhs = [], []
    row_total = jnp.zeros((t_rows, 1), F32)
    mixed = jnp.zeros((t_rows, HD), F32)
    for off in range(reach + 1):
        t = jnp.tanh(dot(query, kv[off, 0], 1, 1) / soft_cap)
        far = gap + off * t_rows
        e = jnp.where((far >= 0) & (far <= limit), jnp.exp(soft_cap * t), 0.0)
        exps.append(e)
        tanhs.append(t)
        row_total = row_total + jnp.sum(e, axis=1, keepdims=True)
        mixed = mixed + dot(e.astype(BF16), kv[off, 1], 1, 0)
    inv_total = 1.0 / row_total
    attn_rows = (mixed * inv_total).astype(BF16)
    attn[...] = attn_rows
    delta = jnp.sum(out_grad.astype(F32) * attn_rows.astype(F32), axis=1, keepdims=True)

    def kg_send(off, which):
        device = (z - off, w if which == 0 else partner)
        return pltpu.make_async_remote_copy(
            src_ref=kvs.at[off, which], dst_ref=kvr.at[off, which], send_sem=kg_s.at[off * 2 + which],
            recv_sem=kg_r.at[off * 2 + which], device_id=device, device_id_type=MESH,
        )

    rot_grad = jnp.zeros((t_rows, HD), F32)
    own = None
    for off in range(reach, -1, -1):
        probs = exps[off] * inv_total
        pg = dot(out_grad, kv[off, 1], 1, 1)
        low = (probs * (pg - delta) * (1.0 - tanhs[off] * tanhs[off])).astype(BF16)
        rot_grad = rot_grad + dot(low, kv[off, 0], 1, 0)
        key_g = dot(low, query, 0, 0)
        val_g = dot(probs.astype(BF16), out_grad, 0, 0)
        own = jnp.where(even, key_g, val_g)
        kvs[off, 1] = jnp.where(even, val_g, key_g).astype(BF16)
        if off == 0:
            pending.append(kg_send(0, 1))
            pending[-1].start()
        else:
            kvs[off, 0] = own.astype(BF16)

            @pl.when(z >= off)
            def _():
                kg_send(off, 0).start()
                kg_send(off, 1).start()

            @pl.when(z + off >= n_seq)
            def _():
                kvr[off] = jnp.zeros((2, t_rows, HD), BF16)

    cot[...] = jnp.zeros_like(cot)
    cot[:t_rows, :HD] = (rot(rot_grad, c_tab, -s_tab) * query_scale).astype(BF16)
    recv(kvr.at[0, 1], kg_s.at[1], kg_r.at[1])
    own = own + kvr[0, 1].astype(F32)
    for off in range(1, reach + 1):

        @pl.when(z + off < n_seq)
        def _():
            recv(kvr.at[off, 0], kg_s.at[off * 2], kg_r.at[off * 2])
            recv(kvr.at[off, 1], kg_s.at[off * 2 + 1], kg_r.at[off * 2 + 1])

        own = own + kvr[off, 0].astype(F32) + kvr[off, 1].astype(F32)
    cot[:t_rows, HD:] = jnp.where(even, rot(own, c_tab, -s_tab), own).astype(BF16)

    for o in range(n_wt):
        for r in range(CAP):
            g = dot(nblk[arrp_sm[o, CAP + r, 0]], cot[...], 1, 0)
            g = jnp.where(arrp[o, r : r + 1, :] >= RB, g[:, BLK:], g[:, :BLK]).astype(BF16)
            for j in range(BLK // chunk):
                wz[r * (BLK // chunk) + j, o * chunk : (o + 1) * chunk, :] = g[j * chunk : (j + 1) * chunk]
    for d in range(1, n_seq):
        pending.append(send(wz.at[to_seq(d)], wzr.at[d], wz_s.at[d], wz_r.at[d], (to_seq(d), w)))

    for d in range(1, n_wt):
        o = to_wt(d)
        gs[frows(o), :] = dot(wd[frows(o), :], cot[...], 1, 1).astype(BF16)
        pending.append(send(gs.at[frows(o)], gr.at[d], g_s.at[d], g_r.at[d], (z, o)))
    ngT[...] = dot(wd[frows(w), :], cot[...], 1, 1)

    part = wz[z].astype(F32)
    for d in range(1, n_seq):
        recv(wzr.at[d], wz_s.at[d], wz_r.at[d])
        part = part + wzr[d].astype(F32)
    ws[...] = part.astype(BF16)

    def crows(i):
        return pl.ds(pl.multiple_of(i * chunk, 16), chunk)

    for d in range(1, n_wt):
        o = to_wt(d)
        pending.append(send(ws.at[crows(o)], fin.at[z * n_wt + w], ow_s.at[d], ow_r.at[d], (z, o)))
    fin[z * n_wt + w] = ws[crows(w), :]

    for d in range(1, n_wt):
        recv(gr.at[d], g_s.at[d], g_r.at[d])
        ngT[...] += gr[d].astype(F32)
    weighted = ngT[...] * scT[...]
    rd[0] = jnp.broadcast_to(jnp.sum(weighted * gain[...], axis=0, keepdims=True), (8, TP))
    for d in range(1, n_wt):
        pending.append(send(rd.at[0], rd.at[d], rd_s.at[d], rd_r.at[d], (z, to_wt(d))))

    for d in range(1, n_wt):
        recv(fin.at[z * n_wt + from_wt(d)], ow_s.at[d], ow_r.at[d])
    for d in range(1, n_seq):
        pending.append(send(fin.at[pl.ds(z * n_wt, n_wt)], fin.at[pl.ds(z * n_wt, n_wt)], fi_s.at[d], fi_r.at[d], (to_seq(d), w)))

    tokT[:feats, :128] = jnp.broadcast_to(jnp.sum(weighted, axis=1, keepdims=True), (feats, 128))
    gb[0] = tokT[:, :128].T[:8, :].astype(BF16).astype(F32)
    for d in range(1, n_seq):
        pending.append(send(gb.at[0], gb.at[d], gb_s.at[d], gb_r.at[d], (to_seq(d), w)))

    for d in range(1, n_wt):
        recv(rd.at[d], rd_s.at[d], rd_r.at[d])
    dots = rd[0]
    for d in range(1, n_wt):
        dots = dots + rd[d]
    dots_row = dots[0:1, :] / D
    tokT[:feats, :] = inv_row * (ngT[...] * gain[...] - scT[...] * dots_row)
    tg[...] = tokT[...].T[:t_rows, :feats].astype(BF16)

    for d in range(1, n_seq):
        recv(gb.at[d], gb_s.at[d], gb_r.at[d])
    sums = gb[0]
    for d in range(1, n_seq):
        sums = sums + gb[d]
    gg[...] = sums

    for d in range(1, n_seq):
        recv(fin.at[pl.ds(from_seq(d) * n_wt, n_wt)], fi_s.at[d], fi_r.at[d])
    per = BLK // chunk
    for s in range(slots):
        for j in range(per):
            bg[s, j * chunk : (j + 1) * chunk, :] = fin[dest[s * per + j]]

    for copy in pending:
        copy.wait_send()
    for off in range(1, reach + 1):

        @pl.when(z + off < n_seq)
        def _():
            kv_send(off, 0).wait_send()
            kv_send(off, 1).wait_send()

        @pl.when(z >= off)
        def _():
            kg_send(off, 0).wait_send()
            kg_send(off, 1).wait_send()


def body(tokens_in, norm_gain, positions, blocks, slot_code, out_grad):
    t_rows, feats = tokens_in.shape
    n_wt = lax.axis_size("wt")
    n_seq = lax.axis_size("seq")
    slots = blocks.shape[1]
    count = n_wt * CAP
    reach = n_seq // 2
    chunk = CAP * BLK // n_seq
    fp = -(-feats // 128) * 128
    half = HD // 2
    frequency = 10000.0 ** (-2.0 * jnp.arange(half, dtype=F32) / HD)
    angles = positions.astype(F32)[:, None] * frequency[None, :]
    cos, sin = jnp.cos(angles), jnp.sin(angles)
    cos = jnp.concatenate([cos, cos], axis=1)
    sin = jnp.concatenate([-sin, sin], axis=1)
    codes = slot_code[0]
    live = codes >= 0
    user = jnp.where(live, codes // POS, -1)
    ids = jnp.arange(slots, dtype=jnp.int32)
    before = (user[None, :] == user[:, None]) & (ids[None, :] < ids[:, None])
    rank = jnp.sum(before.astype(jnp.int32), axis=1)
    dest = jnp.where(live, user * CAP + rank, -1)
    hit = dest[None, :] == jnp.arange(count, dtype=jnp.int32)[:, None]
    slot_of = jnp.sum(jnp.where(hit, ids[None, :], 0), axis=1)
    spot = jnp.sum(jnp.where(hit, (codes - user * POS + 1)[None, :], 0), axis=1) - 1
    spot = spot.reshape(n_wt, CAP)
    row = jnp.maximum(jnp.where(spot >= RB, spot - RB, spot), 0)
    place = jnp.concatenate([spot, row, jnp.zeros((n_wt, 8 - 2 * CAP), jnp.int32)], axis=1)
    place = jnp.broadcast_to(place[:, :, None], (n_wt, 8, 128))
    per = BLK // chunk
    piece = (rank[:, None] * per + jnp.arange(per, dtype=jnp.int32)[None, :]) * n_wt + user[:, None]
    piece = jnp.where(live[:, None], piece, n_seq * n_wt).reshape(-1)
    vmem = pl.BlockSpec(memory_space=pltpu.VMEM)
    smem = pl.BlockSpec(memory_space=pltpu.SMEM)
    dma = lambda n: pltpu.SemaphoreType.DMA((n,))
    kvn = 2 * (reach + 1)
    attn, tg, gg, bg = pl.pallas_call(
        functools.partial(kernel, n_seq, n_wt),
        out_shape=(
            jax.ShapeDtypeStruct((t_rows, HD), BF16),
            jax.ShapeDtypeStruct((t_rows, feats), BF16),
            jax.ShapeDtypeStruct((8, fp), F32),
            jax.ShapeDtypeStruct((slots, BLK, BLK), BF16),
        ),
        in_specs=[vmem] * 6 + [smem] * 2 + [vmem] * 2,
        out_specs=(vmem,) * 4,
        scratch_shapes=[
            pltpu.VMEM((TP, fp), F32),
            pltpu.VMEM((fp, TP), F32),
            pltpu.VMEM((feats, TP), F32),
            pltpu.VMEM((feats, TP), F32),
            pltpu.VMEM((n_wt, 8, TP), F32),
            pltpu.VMEM((n_wt, 8, TP), F32),
            pltpu.VMEM((D, TP), BF16),
            pltpu.VMEM((count, BLK, BLK), BF16),
            pltpu.VMEM((count + 1, BLK, BLK), BF16),
            pltpu.VMEM((n_wt, 8, 128), jnp.int32),
            pltpu.VMEM((8, 128), jnp.int32),
            pltpu.SMEM((8, 128), jnp.int32),
            pltpu.SMEM((n_wt, 8, 128), jnp.int32),
            pltpu.VMEM((D, 2 * HD), BF16),
            pltpu.VMEM((TP, 2 * HD), F32),
            pltpu.VMEM((reach + 1, 2, t_rows, HD), BF16),
            pltpu.VMEM((reach + 1, 2, t_rows, HD), BF16),
            pltpu.VMEM((reach + 1, 2, t_rows, HD), BF16),
            pltpu.VMEM((TP, 2 * HD), BF16),
            pltpu.VMEM((n_seq, n_wt * chunk, BLK), BF16),
            pltpu.VMEM((n_seq, n_wt * chunk, BLK), BF16),
            pltpu.VMEM((n_wt * chunk, BLK), BF16),
            pltpu.VMEM((n_seq * n_wt + 1, chunk, BLK), BF16),
            pltpu.VMEM((D, TP), BF16),
            pltpu.VMEM((n_wt, feats, TP), BF16),
            pltpu.VMEM((n_seq, 8, fp), F32),
            pltpu.VMEM((RB, BLK, TP), BF16),
        ]
        + [dma(n_wt)] * 8
        + [dma(kvn)] * 4
        + [dma(n_seq)] * 2
        + [dma(n_wt)] * 2
        + [dma(n_seq)] * 2
        + [dma(n_wt)] * 4
        + [dma(n_seq)] * 2
        + [dma(2)],
        compiler_params=pltpu.CompilerParams(
            collective_id=0, has_side_effects=True, vmem_limit_bytes=56 * 1024 * 1024
        ),
    )(
        tokens_in, norm_gain[:, None], positions[:, None], cos, sin, blocks[0],
        slot_of.astype(jnp.int32), piece.astype(jnp.int32), place.astype(jnp.int32), out_grad,
    )
    return attn, tg, gg[0, :feats], bg[None]


def solution(mesh):
    placed = (
        P("seq", "wt"),
        P("wt"),
        P("seq"),
        P("wt", None, None, None),
        P("wt", None),
        P("seq", "wt"),
    )
    return jax.shard_map(
        body,
        mesh=mesh,
        in_specs=placed,
        out_specs=(P("seq", "wt"), P("seq", "wt"), P("wt"), P("wt", None, None, None)),
        check_vma=False,
    )
```

time: 199 us -> 116 us (0.58)
  the two profiles are of different devices: /device:TPU:0 before, /device:TPU:25 now
where the time goes in v1:
time: 116 us; the launch traced here: 115 us
  Pallas kernels  102 us (88%)
  local copies, waits for them, and re-layouts  9.88 us (9%)
  other arithmetic  2.34 us (2%)
    pallas_call x1, Pallas kernels, body(): pl.pallas_call(functools.partial(kernel, n_seq, n_wt), out_shape=(jax.Sha...  102 us
    unnamed x11, local copies, waits for them, and re-layouts  5.26 us

profile of v1, /device:TPU:25, one launch (start us, length us, event | category | flops | bytes accessed | tf_op | source)
XLA Modules:
  0.0 115.4 jit_solution(15212199009218303099)
XLA Ops:
  0.6 0.0 copy-start.3
  0.6 0.6 copy-done.3
  1.3 0.1 pad.2.clone
  1.4 0.0 copy-start.2
  1.4 0.7 copy-done.2
  2.1 0.2 convert_reduce_fusion
  2.3 0.6 select_reduce_fusion
  2.9 0.1 sub.26
  3.0 0.1 sub.29
  3.1 0.1 add_add_fusion
  3.2 0.1 add_select_fusion
  3.2 0.7 select_n.57.dest
  3.9 0.7 broadcast_in_dim.73.place
  4.6 0.0 copy-start.1
  4.6 0.8 copy.13.pos
  5.4 0.0 copy-done.1
  5.4 0.9 broadcast_in_dim.75.gain
  6.3 0.5 fusion
  6.7 0.8 pad_maximum_fusion
  7.6 102.5 %shard_map.93 = (bf16[224,128]{1,0:T(8,128)(2,1)}, bf16[224,576]{1,0:T(8,128)(2,1)}, f32[8,640]{1,0:T(8,128)}, bf16[16,128,128]{2,1,0:T(8,128)(2,1)}) custom-call(bf16[224,576]{1,0:T(8,128)(2,1)} %tok.1, f32[576,1]{1,0:T(8,128)} %broadcast_in_dim.75.gain, s32[224,1]{1,0:T(8,128)} %copy.13.pos, f32[224,128]{1,0:T(8,128)} %get-tuple-element.21.cos, ...), custom_call_target="tpu_custom_call" | custom-call | tf_op jit(solution)/shard_map/pallas_call | solution.py:383
  110.1 0.0 copy-start
  110.1 1.4 %slice_reduce_fusion = f32[576]{0:T(1024)} fusion(f32[8,640]{1,0:T(8,128)} %get-tuple-element.10), kind=kLoop, calls=%fused_computation.15 | loop fusion | bytes 4608 | tf_op jit(solution)/shard_map/slice | solution.py:437
  111.5 1.4 %copy.17 = bf16[224,128]{1,0:T(8,128)(2,1)} copy(bf16[224,128]{1,0:T(8,128)(2,1)} %get-tuple-element.27) | data formatting | bytes 114688
  112.9 1.7 %copy.18 = bf16[224,576]{1,0:T(8,128)(2,1)} copy(bf16[224,576]{1,0:T(8,128)(2,1)} %get-tuple-element.28) | data formatting | bytes 516096
  114.6 0.0 copy-done
  114.6 0.8 copy.19
  (10 shorter events, 0.1 us)
Async XLA Ops:
  0.6 0.7 copy-start.3
  1.4 0.7 copy-start.2
  4.6 0.8 copy-start.1
  110.1 4.5 %copy-start = (bf16[16,128,128]{2,1,0:T(8,128)(2,1)S(1)}, bf16[16,128,128]{2,1,0:T(8,128)(2,1)}, u32[]{:S(2)}) copy-start(bf16[16,128,128]{2,1,0:T(8,128)(2,1)} %get-tuple-element.11) | copy-start | bytes 1572868

commit v2 on v1

--- a/solution.py
+++ b/solution.py
@@ -125,8 +125,9 @@
     scaled = tokT[:feats, :] * inv_row
     scT[...] = scaled
     nT[frows(w), :] = (scaled * gain[...]).astype(BF16)
-    for d in range(1, n_wt):
-        pending.append(send(nT.at[frows(w)], nT.at[frows(w)], nt_s.at[d], nt_r.at[d], (z, to_wt(d))))
+    for d in [*range(2, n_wt, 2), 1]:
+        device = (z, partner) if d == 1 else (z, to_wt(d))
+        pending.append(send(nT.at[frows(w)], nT.at[frows(w)], nt_s.at[d], nt_r.at[d], device))
 
     for d in range(1, n_wt):
         recv(arrp.at[from_wt(d)], pc_s.at[d], pc_r.at[d])
@@ -149,10 +150,21 @@
         wd[p * BLK : (p + 1) * BLK, BLK:] = arrived[inv_sm[0, RB + p]]
 
     proj[...] = dot(nT[frows(w), :], wd[frows(w), :], 0, 0)
-    for d in range(1, n_wt):
+
+    def add_proj(src):
+        proj[...] += dot(nT[frows(src), :], wd[frows(src), :], 0, 0)
+
+    recv(nT.at[frows(partner)], nt_s.at[1], nt_r.at[1])
+    add_proj(partner)
+    for d in range(2, n_wt, 2):
         src = from_wt(d)
         recv(nT.at[frows(src)], nt_s.at[d], nt_r.at[d])
-        proj[...] += dot(nT[frows(src), :], wd[frows(src), :], 0, 0)
+        pending.append(send(nT.at[frows(src)], nT.at[frows(src)], nt_s.at[d + 1], nt_r.at[d + 1], (z, partner)))
+        add_proj(src)
+    for d in range(2, n_wt, 2):
+        src = lax.rem(partner + n_wt - d, n_wt)
+        recv(nT.at[frows(src)], nt_s.at[d + 1], nt_r.at[d + 1])
+        add_proj(src)
 
     query = (rot(proj[:t_rows, :HD], c_tab, s_tab) * query_scale).astype(BF16)
     pair = proj[:t_rows, HD:]
@@ -268,11 +280,21 @@
     for d in range(1, n_seq):
         pending.append(send(wz.at[to_seq(d)], wzr.at[d], wz_s.at[d], wz_r.at[d], (to_seq(d), w)))
 
-    for d in range(1, n_wt):
+    order = [*range(2, n_wt, 2), 0]
+    for d in order:
+        o = lax.rem(partner + d, n_wt)
+        gs[frows(o), :] = dot(wd[frows(o), :], cot[...], 1, 1).astype(BF16)
+        pending.append(send(gs.at[frows(o)], gr.at[d + 1], g_s.at[d + 1], g_r.at[d + 1], (z, partner)))
+    for d in order:
         o = to_wt(d)
-        gs[frows(o), :] = dot(wd[frows(o), :], cot[...], 1, 1).astype(BF16)
-        pending.append(send(gs.at[frows(o)], gr.at[d], g_s.at[d], g_r.at[d], (z, o)))
-    ngT[...] = dot(wd[frows(w), :], cot[...], 1, 1)
+        g = dot(wd[frows(o), :], cot[...], 1, 1)
+        recv(gr.at[d + 1], g_s.at[d + 1], g_r.at[d + 1])
+        g = g + gr[d + 1].astype(F32)
+        if d == 0:
+            ngT[...] = g
+        else:
+            gs[frows(o), :] = g.astype(BF16)
+            pending.append(send(gs.at[frows(o)], gr.at[d], g_s.at[d], g_r.at[d], (z, o)))
 
     part = wz[z].astype(F32)
     for d in range(1, n_seq):
@@ -288,7 +310,7 @@
         pending.append(send(ws.at[crows(o)], fin.at[z * n_wt + w], ow_s.at[d], ow_r.at[d], (z, o)))
     fin[z * n_wt + w] = ws[crows(w), :]
 
-    for d in range(1, n_wt):
+    for d in range(2, n_wt, 2):
         recv(gr.at[d], g_s.at[d], g_r.at[d])
         ngT[...] += gr[d].astype(F32)
     weighted = ngT[...] * scT[...]

time: 116 us -> 95.8 us (0.83)
  the two profiles are of different devices: /device:TPU:25 before, /device:TPU:0 now
where the time goes in v2:
time: 95.8 us; the launch traced here: 95.5 us
  Pallas kernels  82.6 us (86%)
  local copies, waits for them, and re-layouts  9.88 us (10%)
  other arithmetic  2.34 us (2%)
    pallas_call x1, Pallas kernels, body(): pl.pallas_call(functools.partial(kernel, n_seq, n_wt), out_shape=(jax.Sha...  82.6 us
    unnamed x11, local copies, waits for them, and re-layouts  5.26 us

profile of v2, /device:TPU:0, one launch (start us, length us, event | category | flops | bytes accessed | tf_op | source)
XLA Modules:
  0.0 95.5 jit_solution(7405393676624388158)
XLA Ops:
  0.6 0.0 copy-start.3
  0.6 0.6 copy-done.3
  1.3 0.1 pad.2.clone
  1.4 0.0 copy-start.2
  1.4 0.7 copy-done.2
  2.1 0.2 convert_reduce_fusion
  2.3 0.6 select_reduce_fusion
  2.9 0.1 sub.26
  3.0 0.1 sub.29
  3.1 0.1 add_add_fusion
  3.2 0.1 add_select_fusion
  3.2 0.7 select_n.57.dest
  3.9 0.7 broadcast_in_dim.73.place
  4.6 0.0 copy-start.1
  4.6 0.8 copy.13.pos
  5.4 0.0 copy-done.1
  5.4 0.9 broadcast_in_dim.75.gain
  6.3 0.5 fusion
  6.7 0.8 pad_maximum_fusion
  7.6 82.6 %shard_map.93 = (bf16[224,128]{1,0:T(8,128)(2,1)}, bf16[224,576]{1,0:T(8,128)(2,1)}, f32[8,640]{1,0:T(8,128)}, bf16[16,128,128]{2,1,0:T(8,128)(2,1)}) custom-call(bf16[224,576]{1,0:T(8,128)(2,1)} %tok.1, f32[576,1]{1,0:T(8,128)} %broadcast_in_dim.75.gain, s32[224,1]{1,0:T(8,128)} %copy.13.pos, f32[224,128]{1,0:T(8,128)} %get-tuple-element.21.cos, ...), custom_call_target="tpu_custom_call" | custom-call | tf_op jit(solution)/shard_map/pallas_call | solution.py:405
  90.2 0.0 copy-start
  90.2 1.4 %slice_reduce_fusion = f32[576]{0:T(1024)} fusion(f32[8,640]{1,0:T(8,128)} %get-tuple-element.10), kind=kLoop, calls=%fused_computation.15 | loop fusion | bytes 4608 | tf_op jit(solution)/shard_map/slice | solution.py:459
  91.6 1.4 %copy.17 = bf16[224,128]{1,0:T(8,128)(2,1)} copy(bf16[224,128]{1,0:T(8,128)(2,1)} %get-tuple-element.27) | data formatting | bytes 114688
  93.0 1.7 %copy.18 = bf16[224,576]{1,0:T(8,128)(2,1)} copy(bf16[224,576]{1,0:T(8,128)(2,1)} %get-tuple-element.28) | data formatting | bytes 516096
  94.7 0.0 copy-done
  94.7 0.8 copy.19
  (10 shorter events, 0.1 us)
Async XLA Ops:
  0.6 0.7 copy-start.3
  1.4 0.7 copy-start.2
  4.6 0.8 copy-start.1
  90.2 4.5 %copy-start = (bf16[16,128,128]{2,1,0:T(8,128)(2,1)S(1)}, bf16[16,128,128]{2,1,0:T(8,128)(2,1)}, u32[]{:S(2)}) copy-start(bf16[16,128,128]{2,1,0:T(8,128)(2,1)} %get-tuple-element.11) | copy-start | bytes 1572868

commit v3 on v2

--- a/solution.py
+++ b/solution.py
@@ -173,9 +173,9 @@
     kv_out = []
 
     def kv_send(off, which):
-        device = (z + off, w if which == 0 else partner)
+        device = (z + off, w) if which == 0 else (z, partner)
         return pltpu.make_async_remote_copy(
-            src_ref=kv.at[0, par], dst_ref=kv.at[off, par], send_sem=kv_s.at[off * 2 + which],
+            src_ref=kv.at[0 if which == 0 else off, par], dst_ref=kv.at[off, par], send_sem=kv_s.at[off * 2 + which],
             recv_sem=kv_r.at[off * 2 + which], device_id=device, device_id_type=MESH,
         )
 
@@ -186,7 +186,6 @@
         @pl.when(z + off < n_seq)
         def _():
             kv_send(off, 0).start()
-            kv_send(off, 1).start()
 
         @pl.when(z < off)
         def _():
@@ -202,6 +201,12 @@
         @pl.when(z >= off)
         def _():
             recv(kv.at[off, par], kv_s.at[off * 2], kv_r.at[off * 2])
+            kv_send(off, 1).start()
+
+    for off in range(1, reach + 1):
+
+        @pl.when(z >= off)
+        def _():
             recv(kv.at[off, 1 - par], kv_s.at[off * 2 + 1], kv_r.at[off * 2 + 1])
 
     gap = lax.broadcasted_iota(jnp.int32, (t_rows, t_rows), 0) - lax.broadcasted_iota(
@@ -358,10 +363,10 @@
         @pl.when(z + off < n_seq)
         def _():
             kv_send(off, 0).wait_send()
+
+        @pl.when(z >= off)
+        def _():
             kv_send(off, 1).wait_send()
-
-        @pl.when(z >= off)
-        def _():
             kg_send(off, 0).wait_send()
             kg_send(off, 1).wait_send()
 

time: 95.8 us -> 95.6 us (level)
  no operation moved by 1% of the time
where the time goes in v3:
time: 95.6 us; the launch traced here: 94.9 us
  Pallas kernels  82 us (86%)
  local copies, waits for them, and re-layouts  9.88 us (10%)
  other arithmetic  2.34 us (2%)
    pallas_call x1, Pallas kernels, body(): pl.pallas_call(functools.partial(kernel, n_seq, n_wt), out_shape=(jax.Sha...  82 us
    unnamed x11, local copies, waits for them, and re-layouts  5.26 us

profile of v3, /device:TPU:0, one launch (start us, length us, event | category | flops | bytes accessed | tf_op | source)
XLA Modules:
  0.0 94.9 jit_solution(11364445218570729470)
XLA Ops:
  0.6 0.0 copy-start.3
  0.6 0.6 copy-done.3
  1.3 0.1 pad.2.clone
  1.4 0.0 copy-start.2
  1.4 0.7 copy-done.2
  2.1 0.2 convert_reduce_fusion
  2.3 0.6 select_reduce_fusion
  2.9 0.1 sub.26
  3.0 0.1 sub.29
  3.1 0.1 add_add_fusion
  3.2 0.1 add_select_fusion
  3.2 0.7 select_n.57.dest
  3.9 0.7 broadcast_in_dim.73.place
  4.6 0.0 copy-start.1
  4.6 0.8 copy.13.pos
  5.4 0.0 copy-done.1
  5.4 0.9 broadcast_in_dim.75.gain
  6.3 0.5 fusion
  6.7 0.8 pad_maximum_fusion
  7.6 82.0 %shard_map.93 = (bf16[224,128]{1,0:T(8,128)(2,1)}, bf16[224,576]{1,0:T(8,128)(2,1)}, f32[8,640]{1,0:T(8,128)}, bf16[16,128,128]{2,1,0:T(8,128)(2,1)}) custom-call(bf16[224,576]{1,0:T(8,128)(2,1)} %tok.1, f32[576,1]{1,0:T(8,128)} %broadcast_in_dim.75.gain, s32[224,1]{1,0:T(8,128)} %copy.13.pos, f32[224,128]{1,0:T(8,128)} %get-tuple-element.21.cos, ...), custom_call_target="tpu_custom_call" | custom-call | tf_op jit(solution)/shard_map/pallas_call | solution.py:410
  89.6 0.0 copy-start
  89.6 1.4 %slice_reduce_fusion = f32[576]{0:T(1024)} fusion(f32[8,640]{1,0:T(8,128)} %get-tuple-element.10), kind=kLoop, calls=%fused_computation.15 | loop fusion | bytes 4608 | tf_op jit(solution)/shard_map/slice | solution.py:464
  91.0 1.4 %copy.17 = bf16[224,128]{1,0:T(8,128)(2,1)} copy(bf16[224,128]{1,0:T(8,128)(2,1)} %get-tuple-element.27) | data formatting | bytes 114688
  92.4 1.7 %copy.18 = bf16[224,576]{1,0:T(8,128)(2,1)} copy(bf16[224,576]{1,0:T(8,128)(2,1)} %get-tuple-element.28) | data formatting | bytes 516096
  94.1 0.0 copy-done
  94.1 0.8 copy.19
  (10 shorter events, 0.1 us)
Async XLA Ops:
  0.6 0.7 copy-start.3
  1.4 0.7 copy-start.2
  4.6 0.8 copy-start.1
  89.6 4.5 %copy-start = (bf16[16,128,128]{2,1,0:T(8,128)(2,1)S(1)}, bf16[16,128,128]{2,1,0:T(8,128)(2,1)}, u32[]{:S(2)}) copy-start(bf16[16,128,128]{2,1,0:T(8,128)(2,1)} %get-tuple-element.11) | copy-start | bytes 1572868
